TPU v7x, 512 devices: a whole 4x4x16 slice. The times are simulated.
512 devices in a mesh: seq: 128 (over z, y, core), head: 4 (over x).
Axes of the slice: x: 4, y: 4, z: 16, core: 2. Of those that a mesh axis runs over, the one named last changes fastest.
Arguments:
- queries: bfloat16 [32768, 1024], P('seq', 'head'), may hold values from -240 to 240
- keys: bfloat16 [32768, 1024], P('seq', 'head'), may hold values from -7.25 to 7.25
- values: bfloat16 [32768, 1024], P('seq', 'head'), may hold values from -6 to 6
- w_out: bfloat16 [1024, 1024], P('head'), may hold values from -0.1875 to 0.1875
Outputs:
- mixed: bfloat16 [1024, 32768], P('head', 'seq')
All inputs are finite; a program needn't handle non-finite values.
Results may differ from a plain program's by a relative error of at most 0.005.
Values may be sent and summed in bfloat16 or wider, within the bound.
A program may use at most 64 MiB of HBM per device.

v0:
```python
import functools

import jax
import jax.numpy as jnp
from jax import lax
from jax.experimental import pallas as pl
from jax.experimental.pallas import tpu as pltpu
from jax.sharding import PartitionSpec as P

HEAD_DIM = 64
BLOCK = 128
LEVELS = 6
HALF = BLOCK // 2
F32 = jnp.float32
BF16 = jnp.bfloat16
MESH = pl.DeviceIdType.MESH
FAR = (3, 4, 5, 6)
OFF = -1e30
EARLY, MIDDLE, LATE = 4, 6, 8


def dot(a, b):
    return jnp.dot(a, b, preferred_element_type=F32)


def iota(shape, dim):
    return lax.broadcasted_iota(jnp.int32, shape, dim)


def pool(rows, fine, level, repeat):
    r, c = iota((rows, fine), 0), iota((rows, fine), 1)
    hit = (c >> level) == (r & (repeat - 1))
    return jnp.where(hit, 2.0**-level, 0.0).astype(BF16)


def unpack(n):
    r, c = iota((256, 256), 0), iota((256, 256), 1)
    group, inside = r >> 6, r & 63
    source, row = inside // n, inside & (n - 1)
    return jnp.where(c == source * (4 * n) + group * n + row, 1.0, 0.0).astype(BF16)


def scores_top(s, slabs):
    top = None
    for start, rows, bias in slabs:
        m = jnp.max(s[start : start + rows], axis=0, keepdims=True)
        if bias is not None:
            m = m + bias
        top = m if top is None else jnp.maximum(top, m)
    return top


def attend(k, vt, q, slabs):
    s = dot(k, q)
    top = scores_top(s, slabs)
    parts, total = [], None
    for start, rows, bias in slabs:
        shift = top if bias is None else top - bias
        p = jnp.exp(s[start : start + rows] - shift)
        t = jnp.sum(p, axis=0, keepdims=True)
        total = t if total is None else total + t
        parts.append(p.astype(BF16))
    o = dot(vt, jnp.concatenate(parts, 0))
    o = jnp.concatenate([o[:HEAD_DIM, :BLOCK], o[HEAD_DIM:, BLOCK:]], 1)
    return top, total, o


def merge(a, b):
    top = jnp.maximum(a[0], b[0])
    fa, fb = jnp.exp(a[0] - top), jnp.exp(b[0] - top)
    return top, a[1] * fa + b[1] * fb, a[2] * fa + b[2] * fb


def kernel(
    devices, heads,
    q_hbm, k_hbm, v_hbm, w_hbm, out_ref,
    q_ref, k_ref, v_ref, w_ref, rim, near, g2, g3, g4, g5, g6, s2, s3, s4, s5, s6,
    qbd, kb, vbt, kc, vct, kd, vdt, wt, own_part, part, got, st_m, st_l, st_o, grants, in_s,
    p1_s, p1_r, p2_s, p2_r, p3_s, p3_r, near_s, near_r, part_s, part_r,
):
    d = lax.axis_index("seq")
    x = lax.axis_index("head")
    core = d % 2
    gathers = {3: g3, 4: g4, 5: g5, 6: g6}
    stages = {2: s2, 3: s3, 4: s4, 5: s5, 6: s6}

    def seq(steps):
        return (d + steps + 2 * devices) % devices

    def group(level):
        return 2 ** (level - 2)

    def far_steps(level, p):
        g = group(level)
        if p == 0:
            return 2 * g
        if p == 1:
            return -2 * g
        return (3 - 6 * ((d // g) % 2)) * g

    def remote(src, dst, send, recv, axis, target):
        return pltpu.make_async_remote_copy(
            src_ref=src, dst_ref=dst, send_sem=send, recv_sem=recv,
            device_id={axis: target}, device_id_type=MESH,
        )

    def far_target(level, p):
        target = seq(far_steps(level, p))
        if level == 4 and p == 2:
            target = target + 2 - 4 * ((target // 2) % 2)
        return target

    def phase1(level, p):
        at = (level - 2, p)
        rank = (d % group(level)) // 2
        if level == 2:
            dst = g2.at[p]
        elif level == 4 and p == 2:
            dst = g4.at[1 - rank, core, p]
        else:
            dst = gathers[level].at[rank, core, p]
        return remote(stages[level], dst, p1_s.at[at], p1_r.at[at], "seq", far_target(level, p))

    def phase2_target(level, j):
        chips = group(level) // 2
        mine = (d // 2) % chips
        return d - 2 * mine + 2 * ((mine + j) % chips)

    def phase2(level, j):
        slot = {4: 0, 5: 1, 6: 4}[level] + j - 1
        block = gathers[level].at[(d // 2) % (group(level) // 2), core]
        return remote(block, block, p2_s.at[slot], p2_r.at[slot], "seq", phase2_target(level, j))

    def phase3(level):
        if level == 2:
            src, dst = g2.at[core], g2.at[2]
        else:
            src = dst = gathers[level].at[:, core]
        slot = level - 2
        return remote(src, dst, p3_s.at[slot], p3_r.at[slot], "seq", d + 1 - 2 * core)

    def neighbour(up):
        side = 0 if up else 1
        return remote(
            rim.at[side], near.at[side], near_s.at[side], near_r.at[side], "seq", seq(1 if up else -1)
        )

    def share(b, t):
        at = (b, t - 1)
        return remote(part.at[b, t - 1], got.at[t - 1, b], part_s.at[at], part_r.at[at], "head", (x + t) % heads)

    all1 = [(level, p) for level in (6, 5, 4, 3, 2) for p in range(3 if level > 2 else 2)]
    all2 = [(level, j) for level in (4, 5, 6) for j in range(1, group(level) // 2)]

    def pass_on(level):
        for other, j in all2:
            if other == level:
                phase2(level, j).start()

    def passed(level):
        for other, j in all2:
            if other == level:
                phase2(level, j).wait_recv()

    back = (1, 0, 2)
    relations = {}
    for level, p in all1:
        there = d // group(level) + far_steps(level, p) // group(level)
        inside = (there >= 0) & (there < devices // group(level))
        relations["far", level, p] = ("seq", far_target(level, p), ("far", level, back[p]), inside)
    for up in (True, False):
        inside = d < devices - 1 if up else d > 0
        relations["near", up] = ("seq", seq(1 if up else -1), ("near", not up), inside)
    for j in range(1, 8):
        relations["mate", j] = ("seq", phase2_target(6, j), ("mate", 8 - j), True)
    for t in range(1, heads):
        relations["head", t] = ("head", (x + t) % heads, ("head", heads - t), True)
    slots = {name: i for i, name in enumerate(relations)}
    inside = {name: relation[3] for name, relation in relations.items()}
    above, below = {}, {}
    for name, (axis, target, _, valid) in relations.items():
        here = d if axis == "seq" else x
        above[name] = (target > here) & valid
        below[name] = (target < here) & valid

    def on(condition, *steps):
        @pl.when(condition)
        def _():
            for step in steps:
                step()

    def signal(semaphore, name):
        axis, target = relations[name][:2]
        pl.semaphore_signal(semaphore, inc=1, device_id={axis: target}, device_id_type=MESH)

    def granted(name, *steps):
        on(above[name], lambda: pl.semaphore_wait(grants.at[slots[name]], 1), *steps)

    def arrived(level, p):
        on(inside["far", level, back[p]], lambda: phase1(level, p).wait_recv())

    loads = [
        pltpu.make_async_copy(src, dst, in_s.at[i])
        for i, (src, dst) in enumerate(
            [(k_hbm, k_ref), (v_hbm, v_ref), (q_hbm, q_ref), (w_hbm, w_ref)]
        )
    ]
    loads[0].start()
    loads[1].start()
    barrier = pltpu.get_barrier_semaphore()
    for name in relations:
        on(above[name], lambda: signal(barrier, name))
    loads[2].start()
    loads[3].start()
    count = sum(jnp.where(below[name], 1, 0) for name in relations)
    on(count > 0, lambda: pl.semaphore_wait(barrier, count))
    for name in relations:
        on(below[name], lambda: signal(grants.at[slots[relations[name][2]]], name))

    pools = jnp.concatenate(
        [pool(BLOCK, 256, 1, 128), pool(64, 256, 2, 64), pool(32, 256, 3, 32), pool(16, 256, 4, 16),
         pool(32, 256, 5, 8), pool(16, 256, 6, 4)], 0)
    loads[0].wait()
    loads[1].wait()
    k, v = k_ref[...], v_ref[...]
    ck, cv = dot(pools, k), dot(pools, v)
    blocks = [ck[:, :128], ck[:, 128:], cv[:, :128], cv[:, 128:]]
    for level, start, n in ((2, 128, 64), (3, 192, 32), (4, 224, 16)):
        for c in range(4):
            stages[level][c * n : (c + 1) * n, :] = blocks[c][start : start + n].astype(BF16)
    for level, start, n in ((5, 240, 8), (6, 272, 4)):
        owner = iota((4 * n, 128), 0) // n
        packed = blocks[0][start : start + 4 * n]
        for c in range(1, 4):
            packed = jnp.where(owner == c, blocks[c][start : start + 4 * n], packed)
        stages[level][...] = packed.astype(BF16)
    fine = [k[:, :128], k[:, 128:], v[:, :128], v[:, 128:]]
    for side in range(2):
        edge = BLOCK * (1 - side)
        for c in range(4):
            rim[side, c * BLOCK : (c + 1) * BLOCK, :] = fine[c][edge : edge + BLOCK]
            rim[side, 512 + c * HALF : 512 + (c + 1) * HALF, :] = blocks[c][side * HALF : (side + 1) * HALF].astype(BF16)

    for level, p in all1:
        on(below["far", level, p], lambda: phase1(level, p).start())
    on(below["near", False], lambda: neighbour(False).start())

    def clear(ref):
        ref[...] = jnp.zeros(ref.shape, ref.dtype)

    for level, p in all1:
        slot = g2.at[p] if level == 2 else gathers[level].at[(d % group(level)) // 2, core, p]
        on(jnp.logical_not(inside["far", level, back[p]]), lambda: clear(slot))
    on(d == 0, lambda: clear(near.at[0]))
    on(d == devices - 1, lambda: clear(near.at[1]))
    granted(("near", True), lambda: neighbour(True).start())

    plane = d // 8
    soon, middle, last = plane < MIDDLE, (plane >= MIDDLE) & (plane < LATE), plane >= LATE

    def exchange_if(level, condition):
        for p in range(3 if level > 2 else 2):
            name = ("far", level, p)
            on(
                above[name] & condition,
                lambda: pl.semaphore_wait(grants.at[slots[name]], 1),
                lambda: phase1(level, p).start(),
            )

    for level in (6, 5, 4, 3, 2):
        exchange_if(level, last)

    loads[2].wait()
    qt = (q_ref[...].astype(F32) * HEAD_DIM**-0.5).T
    feature = iota((BLOCK, BLOCK), 0)
    for b in range(2):
        for hp in range(2):
            piece = qt[hp * BLOCK : (hp + 1) * BLOCK, b * BLOCK : (b + 1) * BLOCK]
            low = jnp.where(feature < HEAD_DIM, piece, 0.0)
            high = jnp.where(feature < HEAD_DIM, 0.0, piece)
            qbd[b, hp] = jnp.concatenate([low, high], 1).astype(BF16)

    def keep(u, state):
        st_m[u, 0:1, :], st_l[u, 0:1, :], st_o[u] = state

    def kept(u):
        return st_m[u, 0:1, :], st_l[u, 0:1, :], st_o[u]

    units = [(b, hp) for b in range(2) for hp in range(2)]
    for hp in range(2):
        lanes = slice(hp * BLOCK, (hp + 1) * BLOCK)
        vt = v_ref[:, lanes].T
        kk = k_ref[:, lanes]
        for b in range(2):
            keep(b * 2 + hp, attend(kk, vt, qbd[b, hp], [(0, 256, None)]))

    loads[3].wait()
    for i in range(heads):
        wt[i] = w_ref[:, i * 256 : (i + 1) * 256].T

    def gathered(level):
        for p in range(3 if level > 2 else 2):
            arrived(level, p)

    for level in (2, 3, 4):
        exchange_if(level, jnp.logical_not(last))
    exchange_if(5, middle)
    exchange_if(6, middle)
    for j in range(1, 8):
        granted(("mate", j))

    gathered(2)
    phase3(2).start()
    gathered(3)
    phase3(3).start()
    gathered(4)
    pass_on(4)
    on(inside["near", False], lambda: neighbour(True).wait_recv())
    on(inside["near", True], lambda: neighbour(False).wait_recv())
    half_pool = pool(HALF, BLOCK, 1, HALF)
    lower_ok = jnp.where(d > 0, 0.0, OFF).astype(F32)
    upper_ok = jnp.where(d < devices - 1, 0.0, OFF).astype(F32)

    def far_bias(level):
        g, out = group(level), []
        e, last = d // g, devices // g - 1
        steps = (-2, 2, 3 - 6 * (e % 2))
        for step in steps:
            there = e + step
            out.append(jnp.where((there >= 0) & (there <= last), 0.0, OFF).astype(F32))
        return out

    bias2 = far_bias(2)
    phase3(2).wait_recv()
    for c in range(4):
        kind, hp = c // 2, c % 2
        strip = slice(c * BLOCK, (c + 1) * BLOCK)
        rows = slice(c * HALF, (c + 1) * HALF)
        half = slice(512 + c * HALF, 512 + (c + 1) * HALF)
        pooled = [dot(half_pool, near[side, strip, :]).astype(BF16) for side in range(2)]
        common = [near[0, half, :], near[1, half, :]] + [g2[p, rows, :] for p in range(3)]
        for b in range(2):
            full = jnp.concatenate([near[b, strip, :], pooled[1 - b]] + common, 0)
            if kind == 0:
                kb[b, hp] = full
            else:
                vbt[b, hp] = full.T
    for b, hp in units:
        first, second = (lower_ok, upper_ok) if b == 0 else (upper_ok, lower_ok)
        slabs = [(0, 128, first), (128, 64, second), (192, 64, lower_ok), (256, 64, upper_ok)]
        slabs += [(320 + 64 * p, 64, bias2[p]) for p in range(3)]
        u = b * 2 + hp
        keep(u, merge(kept(u), attend(kb[b, hp], vbt[b, hp], qbd[b, hp], slabs)))
        if u == 1:
            passed(4)
            phase3(4).start()
            exchange_if(5, soon)
            exchange_if(6, soon & (plane >= EARLY))
            gathered(5)
            pass_on(5)
    exchange_if(6, plane < EARLY)
    gathered(6)
    pass_on(6)
    passed(5)
    phase3(5).start()

    def far_chunk(levels, k_to, vt_to):
        slabs, keys, values = [], ([], []), ([], [])
        for level in levels:
            phase3(level).wait_recv()
            n = 256 // 2**level
            g = group(level)
            for p, bias in enumerate(far_bias(level)):
                slabs.append((64 * len(slabs), 64, bias))
                whole = gathers[level][:, :, p].reshape(g, 4 * n, 128)
                if n >= 16:
                    four = [whole[:, c * n : (c + 1) * n, :].reshape(64, 128) for c in range(4)]
                else:
                    moved = dot(unpack(n), whole.reshape(256, 128)).astype(BF16)
                    four = [moved[c * 64 : (c + 1) * 64] for c in range(4)]
                for hp in range(2):
                    keys[hp].append(four[hp])
                    values[hp].append(four[2 + hp])
        for hp in range(2):
            k_to[hp] = jnp.concatenate(keys[hp], 0)
            vt_to[hp] = jnp.concatenate(values[hp], 0).T
        return slabs

    slabs = far_chunk((3, 4), kc, vct)
    for b, hp in units:
        u = b * 2 + hp
        keep(u, merge(kept(u), attend(kc[hp], vct[hp], qbd[b, hp], slabs)))
        if u == 1:
            passed(6)
            phase3(6).start()
    slabs = far_chunk((5,), kd.at[0], vdt.at[0])
    for b, hp in units:
        u = b * 2 + hp
        keep(u, merge(kept(u), attend(kd[0, hp], vdt[0, hp], qbd[b, hp], slabs)))
    for t in range(1, heads):
        granted(("head", t))
    slabs = far_chunk((6,), kd.at[1], vdt.at[1])
    for b, hp in units:
        u = b * 2 + hp
        _, total, o = merge(kept(u), attend(kd[1, hp], vdt[1, hp], qbd[b, hp], slabs))
        o = (o / total).astype(BF16)
        rows = jnp.concatenate([o[:, :BLOCK], o[:, BLOCK:]], 0)
        if hp == 0:
            upper = rows
            continue
        attended = jnp.concatenate([upper, rows], 0)
        for t in (2, 1, 3):
            part[b, t - 1] = dot(wt[(x + t) % heads], attended).astype(BF16)
            share(b, t).start()
        own_part[b] = dot(wt[x], attended)

    for level, p in all1:
        on(inside["far", level, p], lambda: phase1(level, p).wait_send())
    for level, j in all2:
        phase2(level, j).wait_send()
    for level in (2,) + FAR:
        phase3(level).wait_send()
    for up in (True, False):
        on(inside["near", up], lambda: neighbour(up).wait_send())

    for b in range(2):
        total = own_part[b]
        for t in (1, 3, 2):
            share(b, t).wait_recv()
            total = total + got[t - 1, b].astype(F32)
        out_ref[:, b * BLOCK : (b + 1) * BLOCK] = total.astype(BF16)

    for b in range(2):
        for t in range(1, heads):
            share(b, t).wait_send()


def solution(mesh):
    devices, heads = mesh.shape["seq"], mesh.shape["head"]

    def shards(q, k, v, w):
        rows, width = q.shape
        lanes = w.shape[1] // heads
        vmem = pl.BlockSpec(memory_space=pltpu.VMEM)
        dma = pltpu.SemaphoreType.DMA

        def gather(level):
            return pltpu.VMEM((2 ** (level - 3), 2, 3, 4 * (rows >> level), 128), BF16)

        def stage(level):
            return pltpu.VMEM((4 * (rows >> level), 128), BF16)

        return pl.pallas_call(
            functools.partial(kernel, devices, heads),
            out_shape=jax.ShapeDtypeStruct((lanes, rows), BF16),
            in_specs=[pl.BlockSpec(memory_space=pltpu.HBM)] * 4,
            out_specs=vmem,
            scratch_shapes=[
                pltpu.VMEM((rows, width), BF16),
                pltpu.VMEM((rows, width), BF16),
                pltpu.VMEM((rows, width), BF16),
                pltpu.VMEM((width, heads * lanes), BF16),
                pltpu.VMEM((2, 4 * (BLOCK + HALF), 128), BF16),
                pltpu.VMEM((2, 4 * (BLOCK + HALF), 128), BF16),
                pltpu.VMEM((3, 4 * HALF, 128), BF16),
                gather(3), gather(4), gather(5), gather(6),
                stage(2), stage(3), stage(4), stage(5), stage(6),
                pltpu.VMEM((2, 2, 128, 256), BF16),
                pltpu.VMEM((2, 2, 512, 128), BF16),
                pltpu.VMEM((2, 2, 128, 512), BF16),
                pltpu.VMEM((2, 384, 128), BF16),
                pltpu.VMEM((2, 128, 384), BF16),
                pltpu.VMEM((2, 2, 192, 128), BF16),
                pltpu.VMEM((2, 2, 128, 192), BF16),
                pltpu.VMEM((heads, lanes, width), BF16),
                pltpu.VMEM((2, lanes, BLOCK), F32),
                pltpu.VMEM((2, heads - 1, lanes, BLOCK), BF16),
                pltpu.VMEM((heads - 1, 2, lanes, BLOCK), BF16),
                pltpu.VMEM((4, 8, 256), F32),
                pltpu.VMEM((4, 8, 256), F32),
                pltpu.VMEM((4, HEAD_DIM, 256), F32),
                pltpu.SemaphoreType.REGULAR((26,)),
                dma((4,)),
                dma((5, 3)), dma((5, 3)), dma((11,)), dma((11,)), dma((5,)), dma((5,)),
                dma((2,)), dma((2,)),
                dma((2, heads - 1)), dma((2, heads - 1)),
            ],
            compiler_params=pltpu.CompilerParams(
                collective_id=0, has_side_effects=True, vmem_limit_bytes=55040 * 1024
            ),
            cost_estimate=pl.CostEstimate(
                flops=2_000_000_000, bytes_accessed=1_200_000, transcendentals=1_600_000
            ),
        )(q, k, v, w)

    placed = (P("seq", "head"), P("seq", "head"), P("seq", "head"), P("head", None))
    return jax.shard_map(
        shards, mesh=mesh, in_specs=placed, out_specs=P("head", "seq"), check_vma=False
    )
```

profile of v0, /device:TPU:128, one launch (start us, length us, event | category | flops | bytes accessed | tf_op | source)
XLA Modules:
  0.0 38.3 jit_solution(4448739048094240755)
XLA Ops:
  0.0 37.6 %shard_map.46 = bf16[256,256]{1,0:T(8,128)(2,1)S(1)} custom-call(bf16[256,256]{1,0:T(8,128)(2,1)} %q_hbm.1, bf16[256,256]{1,0:T(8,128)(2,1)} %k_hbm.1, bf16[256,256]{1,0:T(8,128)(2,1)} %v_hbm.1, bf16[256,1024]{1,0:T(8,128)(2,1)} %w_hbm.1), custom_call_target="tpu_custom_call" | custom-call | flops 2000000000 | bytes 1200000 | tf_op jit(solution)/shard_map/pallas_call | solution.py:453
  37.6 0.7 %copy.6 = bf16[256,256]{1,0:T(8,128)(2,1)} copy(bf16[256,256]{1,0:T(8,128)(2,1)S(1)} %shard_map.46) | data formatting | bytes 262144
where the time goes:
time: 38.4 us; the launch traced here: 38.3 us
  Pallas kernels  37.6 us (98%)
  local copies, waits for them, and re-layouts  0.66 us (2%)
    pallas_call x1, Pallas kernels, shards(): pl.pallas_call(functools.partial(kernel, devices, heads), out_shape=jax.S...  37.6 us

commit v1 on v0

--- a/solution.py
+++ b/solution.py
@@ -267,7 +267,7 @@
                 lambda: phase1(level, p).start(),
             )
 
-    for level in (6, 5, 4, 3, 2):
+    for level in (2, 3, 4, 5):
         exchange_if(level, last)
 
     loads[2].wait()
@@ -305,7 +305,7 @@
     for level in (2, 3, 4):
         exchange_if(level, jnp.logical_not(last))
     exchange_if(5, middle)
-    exchange_if(6, middle)
+    exchange_if(6, middle | last)
     for j in range(1, 8):
         granted(("mate", j))
 

time: 38.4 us -> 38.4 us (level)
  no operation moved by 1% of the time
where the time goes in v1:
time: 38.4 us; the launch traced here: 38.3 us
  Pallas kernels  37.6 us (98%)
  local copies, waits for them, and re-layouts  0.66 us (2%)
    pallas_call x1, Pallas kernels, shards(): pl.pallas_call(functools.partial(kernel, devices, heads), out_shape=jax.S...  37.6 us

profile of v1, /device:TPU:128, one launch (start us, length us, event | category | flops | bytes accessed | tf_op | source)
XLA Modules:
  0.0 38.3 jit_solution(10232270516745960642)
XLA Ops:
  0.0 37.6 %shard_map.46 = bf16[256,256]{1,0:T(8,128)(2,1)S(1)} custom-call(bf16[256,256]{1,0:T(8,128)(2,1)} %q_hbm.1, bf16[256,256]{1,0:T(8,128)(2,1)} %k_hbm.1, bf16[256,256]{1,0:T(8,128)(2,1)} %v_hbm.1, bf16[256,1024]{1,0:T(8,128)(2,1)} %w_hbm.1), custom_call_target="tpu_custom_call" | custom-call | flops 2000000000 | bytes 1200000 | tf_op jit(solution)/shard_map/pallas_call | solution.py:453
  37.6 0.7 %copy.6 = bf16[256,256]{1,0:T(8,128)(2,1)} copy(bf16[256,256]{1,0:T(8,128)(2,1)S(1)} %shard_map.46) | data formatting | bytes 262144

commit v2 on v1

--- a/solution.py
+++ b/solution.py
@@ -355,9 +355,10 @@
             passed(4)
             phase3(4).start()
             exchange_if(5, soon)
-            exchange_if(6, soon & (plane >= EARLY))
             gathered(5)
             pass_on(5)
+        if u == 2:
+            exchange_if(6, soon & (plane >= EARLY))
     exchange_if(6, plane < EARLY)
     gathered(6)
     pass_on(6)

time: 38.4 us -> 39.2 us (1.021)
  the two profiles are of different devices: /device:TPU:128 before, /device:TPU:320 now
where the time goes in v2:
time: 39.2 us; the launch traced here: 39 us
  Pallas kernels  38.4 us (98%)
  local copies, waits for them, and re-layouts  0.66 us (2%)
    pallas_call x1, Pallas kernels, shards(): pl.pallas_call(functools.partial(kernel, devices, heads), out_shape=jax.S...  38.4 us

profile of v2, /device:TPU:320, one launch (start us, length us, event | category | flops | bytes accessed | tf_op | source)
XLA Modules:
  0.0 39.0 jit_solution(12851347470566994491)
XLA Ops:
  0.0 38.4 %shard_map.46 = bf16[256,256]{1,0:T(8,128)(2,1)S(1)} custom-call(bf16[256,256]{1,0:T(8,128)(2,1)} %q_hbm.1, bf16[256,256]{1,0:T(8,128)(2,1)} %k_hbm.1, bf16[256,256]{1,0:T(8,128)(2,1)} %v_hbm.1, bf16[256,1024]{1,0:T(8,128)(2,1)} %w_hbm.1), custom_call_target="tpu_custom_call" | custom-call | flops 2000000000 | bytes 1200000 | tf_op jit(solution)/shard_map/pallas_call | solution.py:454
  38.4 0.7 %copy.6 = bf16[256,256]{1,0:T(8,128)(2,1)} copy(bf16[256,256]{1,0:T(8,128)(2,1)S(1)} %shard_map.46) | data formatting | bytes 262144

commit v3 on v1

--- a/solution.py
+++ b/solution.py
@@ -16,7 +16,7 @@
 MESH = pl.DeviceIdType.MESH
 FAR = (3, 4, 5, 6)
 OFF = -1e30
-EARLY, MIDDLE, LATE = 4, 6, 8
+EARLY, MIDDLE, LATE = 4, 6, 7
 
 
 def dot(a, b):

time: 38.4 us -> 38.4 us (level)
  no operation moved by 1% of the time
where the time goes in v3:
time: 38.4 us; the launch traced here: 38.3 us
  Pallas kernels  37.6 us (98%)
  local copies, waits for them, and re-layouts  0.66 us (2%)
    pallas_call x1, Pallas kernels, shards(): pl.pallas_call(functools.partial(kernel, devices, heads), out_shape=jax.S...  37.6 us

profile of v3, /device:TPU:128, one launch (start us, length us, event | category | flops | bytes accessed | tf_op | source)
XLA Modules:
  0.0 38.3 jit_solution(3113080961901682802)
XLA Ops:
  0.0 37.6 %shard_map.46 = bf16[256,256]{1,0:T(8,128)(2,1)S(1)} custom-call(bf16[256,256]{1,0:T(8,128)(2,1)} %q_hbm.1, bf16[256,256]{1,0:T(8,128)(2,1)} %k_hbm.1, bf16[256,256]{1,0:T(8,128)(2,1)} %v_hbm.1, bf16[256,1024]{1,0:T(8,128)(2,1)} %w_hbm.1), custom_call_target="tpu_custom_call" | custom-call | flops 2000000000 | bytes 1200000 | tf_op jit(solution)/shard_map/pallas_call | solution.py:453
  37.6 0.7 %copy.6 = bf16[256,256]{1,0:T(8,128)(2,1)} copy(bf16[256,256]{1,0:T(8,128)(2,1)S(1)} %shard_map.46) | data formatting | bytes 262144
